TPU v7x, 256 devices: a whole 4x4x8 slice. The times are simulated.
256 devices in a mesh: heads: 32 (over z, x_lo, core), frames: 8 (over y, x_hi).
Axes of the slice: x: 4 (x_hi: 2, x_lo: 2; x = x_hi * 2 + x_lo), y: 4, z: 8, core: 2. Of those that a mesh axis runs over, the one named last changes fastest.
Arguments:
- query: bfloat16 [32768, 4096], P(('frames', 'heads'))
- keys: bfloat16 [32768, 4096], P(('frames', 'heads'))
- values: bfloat16 [32768, 4096], P(('frames', 'heads')), may hold values from -6 to 6
- query_tan: bfloat16 [32768, 4096], P(('frames', 'heads')), may hold values from -6 to 6
- keys_tan: bfloat16 [32768, 4096], P(('frames', 'heads')), may hold values from -6 to 6
- values_tan: bfloat16 [32768, 4096], P(('frames', 'heads')), may hold values from -6 to 6
- neighbors: int32 [128, 4], P('frames'), may hold values from 0 to 127, as said below
Outputs:
- attended: bfloat16 [32768, 4096], P(('frames', 'heads'))
- attended_tan: bfloat16 [32768, 4096], P(('frames', 'heads'))
Inputs may be any that keep to these rules, and one draw needn't show every extreme that they name: `neighbors`: entry 0 of row b is b itself; the other entries are min(max(b + o, 0), 127) for distinct nonzero offsets o between -4 and 4.
All inputs are finite; a program needn't handle non-finite values.
Results may differ from a plain program's by a relative error of at most 0.028.
Values may be sent and summed in bfloat16 or wider, within the bound.
A program may use at most 192 MiB of HBM per device.

v0:
```python
import jax
import jax.numpy as jnp
from jax import lax
from jax.sharding import PartitionSpec as P

BQ = 256
WK = 4
HB = 4


def extended(array, sides, width):
    for axis, dim in sides:
        devices, length = (lax.axis_size(axis), array.shape[dim])
        up = [(i, (i + 1) % devices) for i in range(devices - 1)]
        down = [(j, i) for i, j in up]
        last = lax.slice_in_dim(array, length - width, length, axis=dim)
        initial = lax.slice_in_dim(array, 0, width, axis=dim)
        before = lax.ppermute(last, axis, up)
        after = lax.ppermute(initial, axis, down)
        array = jnp.concatenate([before, array, after], axis=dim)
    return array


def widen_keys(keys_h, values_h, keys_tanh, values_tanh):
    stacked = jnp.stack([keys_h, values_h, keys_tanh, values_tanh], axis=0)
    return extended(stacked, (("frames", 1),), HB * BQ)


def attend(query_h, query_tanh, padded, neighbors):
    rows, width = query_h.shape
    blocks = rows // BQ
    scale = width ** (-0.5)
    tiles = padded.reshape(4, blocks + 2 * HB, BQ, width)
    local = neighbors - lax.axis_index("frames") * blocks + HB
    chosen = tiles[:, local].reshape(4, blocks, WK * BQ, width)
    k_win, v_win, kt_win, vt_win = (chosen[0], chosen[1], chosen[2], chosen[3])
    q_rows = query_h.reshape(blocks, BQ, width)
    qt_rows = query_tanh.reshape(blocks, BQ, width)
    scores = jnp.einsum("nqd,nkd->nqk", q_rows, k_win, preferred_element_type=jnp.float32) * scale
    probs = jax.nn.softmax(scores, axis=-1)
    probs16 = probs.astype(jnp.bfloat16)
    out = jnp.einsum("nqk,nkd->nqd", probs16, v_win, preferred_element_type=jnp.float32)
    score_tan = (
        jnp.einsum("nqd,nkd->nqk", qt_rows, k_win, preferred_element_type=jnp.float32)
        + jnp.einsum("nqd,nkd->nqk", q_rows, kt_win, preferred_element_type=jnp.float32)
    ) * scale
    weighted = probs * score_tan
    mean_tan = jnp.sum(weighted, axis=-1, keepdims=True)
    weighted16 = weighted.astype(jnp.bfloat16)
    tan = (
        jnp.einsum("nqk,nkd->nqd", probs16, vt_win, preferred_element_type=jnp.float32)
        + jnp.einsum("nqk,nkd->nqd", weighted16, v_win, preferred_element_type=jnp.float32)
        - mean_tan * out
    )
    return (
        out.reshape(rows, width).astype(jnp.bfloat16),
        tan.reshape(rows, width).astype(jnp.bfloat16),
    )


def per_device(query, keys, values, query_tan, keys_tan, values_tan, neighbors):
    query_h, keys_h, values_h, query_tanh, keys_tanh, values_tanh = (
        lax.all_to_all(query, "heads", split_axis=1, concat_axis=0, tiled=True),
        lax.all_to_all(keys, "heads", split_axis=1, concat_axis=0, tiled=True),
        lax.all_to_all(values, "heads", split_axis=1, concat_axis=0, tiled=True),
        lax.all_to_all(query_tan, "heads", split_axis=1, concat_axis=0, tiled=True),
        lax.all_to_all(keys_tan, "heads", split_axis=1, concat_axis=0, tiled=True),
        lax.all_to_all(values_tan, "heads", split_axis=1, concat_axis=0, tiled=True),
    )
    padded = widen_keys(keys_h, values_h, keys_tanh, values_tanh)
    out_h, tan_h = attend(query_h, query_tanh, padded, neighbors)
    attended, attended_tan = (
        lax.all_to_all(out_h, "heads", split_axis=0, concat_axis=1, tiled=True),
        lax.all_to_all(tan_h, "heads", split_axis=0, concat_axis=1, tiled=True),
    )
    return (attended, attended_tan)


def solution(mesh):
    return jax.shard_map(
        per_device,
        mesh=mesh,
        in_specs=(
            P(("frames", "heads"), None),
            P(("frames", "heads"), None),
            P(("frames", "heads"), None),
            P(("frames", "heads"), None),
            P(("frames", "heads"), None),
            P(("frames", "heads"), None),
            P("frames", None),
        ),
        out_specs=(P(("frames", "heads"), None), P(("frames", "heads"), None)),
        check_vma=False,
    )
```

profile of v0, /device:TPU:1, one launch (start us, length us, event | category | flops | bytes accessed | tf_op | source)
XLA Modules:
  0.0 396.5 jit_solution(2317756703018230559)
XLA Ops:
  0.6 0.0 copy-start
  0.6 2.4 copy.26
  3.0 11.1 %all-to-all-start = ((bf16[128,32,128]{0,2,1:T(8,128)(2,1)}), bf16[128,32,128]{0,2,1:T(8,128)(2,1)S(1)}, u32[]{:S(2)}, u32[]{:S(2)}) async-start(bf16[128,32,128]{0,2,1:T(8,128)(2,1)} %bitcast), calls=%async_computation | async-start | bytes 2097152 | tf_op jit(solution)/shard_map/all_to_all | solution.py:64
  14.1 2.3 copy.28
  16.3 25.9 %all-to-all-done = bf16[128,32,128]{0,2,1:T(8,128)(2,1)S(1)} async-done(((bf16[128,32,128]{0,2,1:T(8,128)(2,1)}), bf16[128,32,128]{0,2,1:T(8,128)(2,1)S(1)}, u32[]{:S(2)}, u32[]{:S(2)}) %all-to-all-start) | async-done | bytes 1048608 | tf_op jit(solution)/shard_map/all_to_all | solution.py:64
  42.2 4.8 %all-to-all-start.1 = ((bf16[128,32,128]{0,2,1:T(8,128)(2,1)}), bf16[128,32,128]{0,2,1:T(8,128)(2,1)S(1)}, u32[]{:S(2)}, u32[]{:S(2)}) async-start(bf16[128,32,128]{0,2,1:T(8,128)(2,1)} %bitcast.97), calls=%async_computation.1 | async-start | bytes 2097152 | tf_op jit(solution)/shard_map/all_to_all | solution.py:65
  47.0 2.3 copy.30
  49.3 25.9 %all-to-all-done.1 = bf16[128,32,128]{0,2,1:T(8,128)(2,1)S(1)} async-done(((bf16[128,32,128]{0,2,1:T(8,128)(2,1)}), bf16[128,32,128]{0,2,1:T(8,128)(2,1)S(1)}, u32[]{:S(2)}, u32[]{:S(2)}) %all-to-all-start.1) | async-done | bytes 1048608 | tf_op jit(solution)/shard_map/all_to_all | solution.py:65
  75.2 5.6 %all-to-all-start.2 = ((bf16[128,32,128]{0,2,1:T(8,128)(2,1)}), bf16[128,32,128]{0,2,1:T(8,128)(2,1)}, u32[]{:S(2)}, u32[]{:S(2)}) async-start(bf16[128,32,128]{0,2,1:T(8,128)(2,1)} %bitcast.98), calls=%async_computation.2 | async-start | bytes 2097152 | tf_op jit(solution)/shard_map/all_to_all | solution.py:67
  80.8 2.3 copy.32
  83.1 26.0 %all-to-all-done.2 = bf16[128,32,128]{0,2,1:T(8,128)(2,1)} async-done(((bf16[128,32,128]{0,2,1:T(8,128)(2,1)}), bf16[128,32,128]{0,2,1:T(8,128)(2,1)}, u32[]{:S(2)}, u32[]{:S(2)}) %all-to-all-start.2) | async-done | bytes 1048608 | tf_op jit(solution)/shard_map/all_to_all | solution.py:67
  109.0 5.7 %all-to-all-start.3 = ((bf16[128,32,128]{0,2,1:T(8,128)(2,1)}), bf16[128,32,128]{0,2,1:T(8,128)(2,1)}, u32[]{:S(2)}, u32[]{:S(2)}) async-start(bf16[128,32,128]{0,2,1:T(8,128)(2,1)} %bitcast.99), calls=%async_computation.3 | async-start | bytes 2097152 | tf_op jit(solution)/shard_map/all_to_all | solution.py:68
  114.7 1.3 copy_bitcast_fusion.3
  116.0 26.9 %all-to-all-done.3 = bf16[128,32,128]{0,2,1:T(8,128)(2,1)} async-done(((bf16[128,32,128]{0,2,1:T(8,128)(2,1)}), bf16[128,32,128]{0,2,1:T(8,128)(2,1)}, u32[]{:S(2)}, u32[]{:S(2)}) %all-to-all-start.3) | async-done | bytes 1048608 | tf_op jit(solution)/shard_map/all_to_all | solution.py:68
  142.9 5.7 %all-to-all-start.6 = ((bf16[128,32,128]{2,0,1:T(8,128)(2,1)}), bf16[128,32,128]{2,0,1:T(8,128)(2,1)}, u32[]{:S(2)}, u32[]{:S(2)}) async-start(bf16[128,32,128]{2,0,1:T(8,128)(2,1)} %copy_bitcast_fusion.3), calls=%async_computation.6 | async-start | bytes 2097152 | tf_op jit(solution)/shard_map/all_to_all | solution.py:66
  148.6 0.7 copy.27
  149.3 0.0 copy-start.4
  149.3 0.7 copy.29
  149.9 1.6 copy.31
  151.6 2.3 copy.33
  153.8 2.5 pad_maximum_fusion.4
  156.4 5.3 %collective-permute-start = (bf16[4,1024,128]{2,1,0:T(8,128)(2,1)}, bf16[4,1024,128]{2,1,0:T(8,128)(2,1)}, u32[]{:S(2)}, u32[]{:S(2)}) collective-permute-start(bf16[4,1024,128]{2,1,0:T(8,128)(2,1)} %get-tuple-element.6), channel_id=1, source_target_pairs={{0,1},{1,2},{2,3},{3,4},{4,5},{5,6},{6,7},{8,9},{9,10},{10,11},{11... | collective-permute-start | bytes 3145736 | tf_op jit(solution)/shard_map/ppermute | solution.py:18
  161.7 1.3 collective-permute-start.1
  163.0 0.1 copy.34
  163.1 0.1 reshape.66
  163.2 2.6 copy_bitcast_fusion.4
  165.7 11.1 %all-to-all-done.6 = bf16[128,32,128]{2,0,1:T(8,128)(2,1)} async-done(((bf16[128,32,128]{2,0,1:T(8,128)(2,1)}), bf16[128,32,128]{2,0,1:T(8,128)(2,1)}, u32[]{:S(2)}, u32[]{:S(2)}) %all-to-all-start.6) | async-done | bytes 1048608 | tf_op jit(solution)/shard_map/all_to_all | solution.py:66
  176.8 5.7 %all-to-all-start.4 = ((bf16[128,32,128]{2,0,1:T(8,128)(2,1)}), bf16[128,32,128]{2,0,1:T(8,128)(2,1)}, u32[]{:S(2)}, u32[]{:S(2)}) async-start(bf16[128,32,128]{2,0,1:T(8,128)(2,1)} %copy_bitcast_fusion.4), calls=%async_computation.4 | async-start | bytes 2097152 | tf_op jit(solution)/shard_map/all_to_all | solution.py:63
  182.5 8.8 %collective-permute-done = bf16[4,1024,128]{2,1,0:T(8,128)(2,1)} collective-permute-done((bf16[4,1024,128]{2,1,0:T(8,128)(2,1)}, bf16[4,1024,128]{2,1,0:T(8,128)(2,1)}, u32[]{:S(2)}, u32[]{:S(2)}) %collective-permute-start) | collective-permute-done | bytes 1048608 | tf_op jit(solution)/shard_map/ppermute | solution.py:18
  191.3 31.6 %collective-permute-done.1 = bf16[4,1024,128]{2,1,0:T(8,128)(2,1)} collective-permute-done((bf16[4,1024,128]{2,1,0:T(8,128)(2,1)}, bf16[4,1024,128]{2,1,0:T(8,128)(2,1)}, u32[]{:S(2)}, u32[]{:S(2)}) %collective-permute-start.1) | collective-permute-done | bytes 1048608 | tf_op jit(solution)/shard_map/ppermute | solution.py:19
  222.9 8.6 %pad_maximum_fusion = bf16[4,6144,128]{2,1,0:T(8,128)(2,1)} fusion(bf16[4,1024,128]{2,1,0:T(8,128)(2,1)} %collective-permute-done.1, bf16[1,4096,128]{2,1,0:T(8,128)(2,1)} %bitcast.93, bf16[1,4096,128]{2,1,0:T(8,128)(2,1)S(1)} %bitcast.91, bf16[1,4096,128]{2,1,0:T(8,128)(2,1)S(1)} %bitcast.89, bf16[1,4096,128]{2,1,0:T(8,128)(2,1)S(1)} %bitcast.87, ...), kind=kLoop, calls=%fused_computation.14 | loop fusion | flops 37748736 | bytes 12582912 | tf_op jit(solution)/shard_map/concatenate | solution.py:20
  231.4 10.5 %gather_fusion = bf16[64,4,256,128]{3,2,1,0:T(8,128)(2,1)} fusion(bf16[4,24,256,128]{3,2,1,0:T(8,128)(2,1)} %bitcast.78, s32[1024]{0:T(1024)S(1)} %pad_clamp_fusion), kind=kCustom, calls=%fused_computation | custom fusion | bytes 33554688 | tf_op jit(solution)/shard_map/gather | solution.py:35
  241.9 8.3 %copy.55 = bf16[16,4,4,256,128]{4,3,1,0,2:T(8,128)(2,1)S(1)} copy(bf16[16,4,4,256,128]{4,3,2,1,0:T(8,128)(2,1)} %bitcast.79) | data formatting | bytes 33554432 | tf_op jit(solution)/shard_map/gather | solution.py:35
  250.2 6.1 %fusion.13 = (bf16[1,16,4,256,128]{4,3,2,1,0:T(8,128)(2,1)}, bf16[1,16,4,256,128]{4,3,2,1,0:T(8,128)(2,1)}, bf16[1,16,4,256,128]{4,3,2,1,0:T(8,128)(2,1)}, bf16[1,16,4,256,128]{4,3,2,1,0:T(8,128)(2,1)}) fusion(bf16[4,16,4,256,128]{4,3,2,1,0:T(8,128)(2,1)S(1)} %bitcast.80), kind=kLoop, calls=%fused_computation.28 | loop fusion | bytes 33554432 | tf_op jit(solution)/shard_map/slice | solution.py:36
  256.3 10.6 %fusion.17 = f32[16,1024,256]{2,1,0:T(8,128)} fusion(bf16[16,1024,128]{2,1,0:T(8,128)(2,1)} %bitcast.84, bf16[16,256,128]{2,1,0:T(8,128)(2,1)} %bitcast.24), kind=kOutput, calls=%fused_computation.32 | convolution fusion | flops 1073741824 | bytes 22020096 | tf_op jit(solution)/shard_map/nqd,nkd->nqk/dot_general | solution.py:44
  266.9 0.0 all-to-all-done.4
  266.9 10.2 %fusion.14 = (f32[16,256]{1,0:T(8,128)S(1)}, f32[16,256,1024]{1,2,0:T(8,128)}) fusion(bf16[16,1024,128]{2,1,0:T(8,128)(2,1)} %bitcast.85, bf16[16,256,128]{2,1,0:T(8,128)(2,1)} %bitcast.17), kind=kOutput, calls=%fused_computation.29 | convolution fusion | flops 1086325760 | bytes 22036480 | tf_op jit(solution)/shard_map/sub | solution.py:40
  277.2 9.1 %fusion.9 = bf16[16,256,1024]{1,2,0:T(8,128)(2,1)} fusion(f32[16,256,1024]{1,2,0:T(8,128)} %get-tuple-element.9, f32[16,256]{1,0:T(8,128)S(1)} %get-tuple-element.8), kind=kLoop, calls=%fused_computation.13 | loop fusion | flops 8388608 | bytes 25182208 | tf_op jit(solution)/shard_map/convert_element_type | solution.py:41
  286.3 17.3 %fusion.16 = (f32[16,256]{1,0:T(8,128)S(1)}, bf16[16,256,1024]{1,2,0:T(8,128)(2,1)}) fusion(f32[16,1024,256]{2,1,0:T(8,128)} %fusion.17, bf16[16,1024,128]{2,1,0:T(8,128)(2,1)} %bitcast.100, bf16[16,256,128]{2,1,0:T(8,128)(2,1)} %bitcast.17, f32[16,256,1024]{1,2,0:T(8,128)} %get-tuple-element.9, f32[16,256]{1,0:T(8,128)S(1)} %get-tuple-element.8), kind=kOutput, calls=%fused_computation.31 | convolution fusion | flops 1098903552 | bytes 47218688 | tf_op jit(solution)/shard_map/nqd,nkd->nqk/dot_general | solution.py:45
  303.6 8.6 %fusion.6 = f32[16,256,128]{2,1,0:T(8,128)} fusion(bf16[16,1024,128]{2,1,0:T(8,128)(2,1)} %bitcast.81, bf16[16,256,1024]{1,2,0:T(8,128)(2,1)} %get-tuple-element.13), kind=kOutput, calls=%fused_computation.9 | convolution fusion | flops 1073741824 | bytes 14680064 | tf_op jit(solution)/shard_map/nqk,nkd->nqd/dot_general | solution.py:52
  312.2 0.0 copy-done.2
  312.2 4.1 %fusion.15 = (bf16[16,256,128]{2,1,0:T(8,128)(2,1)}, f32[16,256,128]{2,1,0:T(8,128)}) fusion(bf16[16,256,1024]{1,2,0:T(8,128)(2,1)S(1)} %copy-done.2, bf16[16,1024,128]{2,1,0:T(8,128)(2,1)S(1)} %bitcast.82), kind=kOutput, calls=%fused_computation.30 | convolution fusion | flops 1074266112 | bytes 15728640 | tf_op jit(solution)/shard_map/nqk,nkd->nqd/dot_general | solution.py:42
  316.4 8.7 %subtract_convert_fusion = bf16[16,256,128]{2,1,0:T(8,128)(2,1)S(1)} fusion(f32[16,256,128]{2,1,0:T(8,128)} %get-tuple-element.11, f32[16,256,128]{2,1,0:T(8,128)} %fusion.6, bf16[16,256,1024]{1,2,0:T(8,128)(2,1)} %fusion.9, bf16[16,1024,128]{2,1,0:T(8,128)(2,1)} %bitcast.83, f32[16,256]{1,0:T(8,128)S(1)} %get-tuple-element.12), kind=kOutput, calls=%fused_computation.15 | convolution fusion | flops 1075838976 | bytes 17842176 | tf_op jit(solution)/shard_map/nqk,nkd->nqd/dot_general | solution.py:51
  325.1 37.3 %all_to_all.128 = bf16[32,128,128]{2,1,0:T(8,128)(2,1)S(1)} all-to-all(bf16[32,128,128]{2,1,0:T(8,128)(2,1)S(1)} %bitcast.94), channel_id=1, replica_groups=mesh['heads'=32,'frames'=8] {'heads'}, dimensions={0} | all-to-all | bytes 2097152 | tf_op jit(solution)/shard_map/all_to_all | solution.py:74
  362.4 4.8 %all-to-all-start.5 = ((bf16[32,128,128]{2,1,0:T(8,128)(2,1)}), bf16[32,128,128]{2,1,0:T(8,128)(2,1)S(1)}, u32[]{:S(2)}, u32[]{:S(2)}) async-start(bf16[32,128,128]{2,1,0:T(8,128)(2,1)} %bitcast.101), calls=%async_computation.5 | async-start | bytes 2097152 | tf_op jit(solution)/shard_map/all_to_all | solution.py:73
  367.2 1.1 copy_bitcast_fusion.1
  368.3 27.1 %all-to-all-done.5 = bf16[32,128,128]{2,1,0:T(8,128)(2,1)S(1)} async-done(((bf16[32,128,128]{2,1,0:T(8,128)(2,1)}), bf16[32,128,128]{2,1,0:T(8,128)(2,1)S(1)}, u32[]{:S(2)}, u32[]{:S(2)}) %all-to-all-start.5) | async-done | bytes 1048608 | tf_op jit(solution)/shard_map/all_to_all | solution.py:73
  395.4 1.1 copy_bitcast_fusion.2
  (9 shorter events, 0.0 us)
Async XLA Ops:
  0.6 114.1 %copy-start = (bf16[128,4096]{1,0:T(8,128)(2,1)S(1)}, bf16[128,4096]{1,0:T(8,128)(2,1)}, u32[]{:S(2)}) copy-start(bf16[128,4096]{1,0:T(8,128)(2,1)} %param.10) | copy-start | bytes 3145732
  3.0 39.2 %all-to-all-start = ((bf16[128,32,128]{0,2,1:T(8,128)(2,1)}), bf16[128,32,128]{0,2,1:T(8,128)(2,1)S(1)}, u32[]{:S(2)}, u32[]{:S(2)}) async-start(bf16[128,32,128]{0,2,1:T(8,128)(2,1)} %bitcast), calls=%async_computation | async-start | bytes 2097152 | tf_op jit(solution)/shard_map/all_to_all | solution.py:64
  42.2 33.0 %all-to-all-start.1 = ((bf16[128,32,128]{0,2,1:T(8,128)(2,1)}), bf16[128,32,128]{0,2,1:T(8,128)(2,1)S(1)}, u32[]{:S(2)}, u32[]{:S(2)}) async-start(bf16[128,32,128]{0,2,1:T(8,128)(2,1)} %bitcast.97), calls=%async_computation.1 | async-start | bytes 2097152 | tf_op jit(solution)/shard_map/all_to_all | solution.py:65
  75.2 33.9 %all-to-all-start.2 = ((bf16[128,32,128]{0,2,1:T(8,128)(2,1)}), bf16[128,32,128]{0,2,1:T(8,128)(2,1)}, u32[]{:S(2)}, u32[]{:S(2)}) async-start(bf16[128,32,128]{0,2,1:T(8,128)(2,1)} %bitcast.98), calls=%async_computation.2 | async-start | bytes 2097152 | tf_op jit(solution)/shard_map/all_to_all | solution.py:67
  109.0 33.9 %all-to-all-start.3 = ((bf16[128,32,128]{0,2,1:T(8,128)(2,1)}), bf16[128,32,128]{0,2,1:T(8,128)(2,1)}, u32[]{:S(2)}, u32[]{:S(2)}) async-start(bf16[128,32,128]{0,2,1:T(8,128)(2,1)} %bitcast.99), calls=%async_computation.3 | async-start | bytes 2097152 | tf_op jit(solution)/shard_map/all_to_all | solution.py:68
  142.9 33.9 %all-to-all-start.6 = ((bf16[128,32,128]{2,0,1:T(8,128)(2,1)}), bf16[128,32,128]{2,0,1:T(8,128)(2,1)}, u32[]{:S(2)}, u32[]{:S(2)}) async-start(bf16[128,32,128]{2,0,1:T(8,128)(2,1)} %copy_bitcast_fusion.3), calls=%async_computation.6 | async-start | bytes 2097152 | tf_op jit(solution)/shard_map/all_to_all | solution.py:66
  149.3 13.7 %copy-start.4 = (s32[16,4]{0,1:T(4,128)S(1)}, s32[16,4]{0,1:T(4,128)}, u32[]{:S(2)}) copy-start(s32[16,4]{0,1:T(4,128)} %param.13) | copy-start | bytes 772
  156.4 34.9 %collective-permute-start = (bf16[4,1024,128]{2,1,0:T(8,128)(2,1)}, bf16[4,1024,128]{2,1,0:T(8,128)(2,1)}, u32[]{:S(2)}, u32[]{:S(2)}) collective-permute-start(bf16[4,1024,128]{2,1,0:T(8,128)(2,1)} %get-tuple-element.6), channel_id=1, source_target_pairs={{0,1},{1,2},{2,3},{3,4},{4,5},{5,6},{6,7},{8,9},{9,10},{10,11},{11... | collective-permute-start | bytes 3145736 | tf_op jit(solution)/shard_map/ppermute | solution.py:18
  161.7 61.2 %collective-permute-start.1 = (bf16[4,1024,128]{2,1,0:T(8,128)(2,1)}, bf16[4,1024,128]{2,1,0:T(8,128)(2,1)}, u32[]{:S(2)}, u32[]{:S(2)}) collective-permute-start(bf16[4,1024,128]{2,1,0:T(8,128)(2,1)} %get-tuple-element.7), channel_id=1, source_target_pairs={{1,0},{2,1},{3,2},{4,3},{5,4},{6,5},{7,6},{9,8},{10,9},{11,10},{12... | collective-permute-start | bytes 3145736 | tf_op jit(solution)/shard_map/ppermute | solution.py:19
  176.8 90.1 %all-to-all-start.4 = ((bf16[128,32,128]{2,0,1:T(8,128)(2,1)}), bf16[128,32,128]{2,0,1:T(8,128)(2,1)}, u32[]{:S(2)}, u32[]{:S(2)}) async-start(bf16[128,32,128]{2,0,1:T(8,128)(2,1)} %copy_bitcast_fusion.4), calls=%async_computation.4 | async-start | bytes 2097152 | tf_op jit(solution)/shard_map/all_to_all | solution.py:63
  303.6 8.6 %copy-start.2 = (bf16[16,256,1024]{1,2,0:T(8,128)(2,1)S(1)}, bf16[16,256,1024]{1,2,0:T(8,128)(2,1)}, u32[]{:S(2)}) copy-start(bf16[16,256,1024]{1,2,0:T(8,128)(2,1)} %fusion.9) | copy-start | bytes 25165828
  303.6 8.6 %copy-start.3 = (bf16[1,16,4,256,128]{4,3,2,1,0:T(8,128)(2,1)S(1)}, bf16[1,16,4,256,128]{4,3,2,1,0:T(8,128)(2,1)}, u32[]{:S(2)}) copy-start(bf16[1,16,4,256,128]{4,3,2,1,0:T(8,128)(2,1)} %get-tuple-element.3) | copy-start | bytes 12582916
  316.4 80.2 %copy-start.1 = (bf16[128,4096]{1,0:T(8,128)(2,1)S(1)}, bf16[128,4096]{1,0:T(8,128)(2,1)}, u32[]{:S(2)}) copy-start(bf16[128,4096]{1,0:T(8,128)(2,1)} %param.10) | copy-start | bytes 3145732
  362.4 33.0 %all-to-all-start.5 = ((bf16[32,128,128]{2,1,0:T(8,128)(2,1)}), bf16[32,128,128]{2,1,0:T(8,128)(2,1)S(1)}, u32[]{:S(2)}, u32[]{:S(2)}) async-start(bf16[32,128,128]{2,1,0:T(8,128)(2,1)} %bitcast.101), calls=%async_computation.5 | async-start | bytes 2097152 | tf_op jit(solution)/shard_map/all_to_all | solution.py:73
where the time goes:
time: 398 us; the launch traced here: 397 us
  waiting for transfers between devices  183 us (46%)
  matrix products  59.6 us (15%)
  starting transfers between devices  49.8 us (13%)
  local copies, waits for them, and re-layouts  45.6 us (11%)
  blocking collectives  37.3 us (9%)
  other arithmetic  20.2 us (5%)
    all_to_all x1, blocking collectives, per_device(): lax.all_to_all(tan_h, 'heads', split_axis=0, concat_axis=1, tiled=True)  37.3 us
    ppermute x1, waiting for transfers between devices, extended(): after = lax.ppermute(initial, axis, down)  31.6 us
    all_to_all x1, waiting for transfers between devices, per_device(): lax.all_to_all(out_h, 'heads', split_axis=0, concat_axis=1, tiled=True)  27.1 us
    all_to_all x1, waiting for transfers between devices, per_device(): lax.all_to_all(values_tan, 'heads', split_axis=1, concat_axis=0, tiled=True)  26.9 us
    all_to_all x1, waiting for transfers between devices, per_device(): lax.all_to_all(keys_tan, 'heads', split_axis=1, concat_axis=0, tiled=True)  26 us
    all_to_all x1, waiting for transfers between devices, per_device(): lax.all_to_all(values, 'heads', split_axis=1, concat_axis=0, tiled=True)  25.9 us
    all_to_all x1, waiting for transfers between devices, per_device(): lax.all_to_all(keys, 'heads', split_axis=1, concat_axis=0, tiled=True)  25.9 us
    gather x2, local copies, waits for them, and re-layouts, attend(): chosen = tiles[:, local].reshape(4, blocks, WK * BQ, width)  18.8 us
  transfers between devices with their start and end apart: 9, of which 8 were waited for; matrix products, arithmetic and copies ran while one was open for 16% of the time, Pallas kernels for 0%

commit v1 on v0

v1 whole, which is shorter than its diff:
```python
import functools

import jax
import jax.numpy as jnp
from jax import lax
from jax.experimental import pallas as pl
from jax.experimental.pallas import tpu as pltpu
from jax.sharding import PartitionSpec as P

MESH = pl.DeviceIdType.MESH
HD = 128
BQ = 256
WK = 4
HB = 4
HALO = HB * BQ
HEADS = 32
FRAMES = 8
PLANES = 8
TOK = 128
ROWS = HEADS * TOK
PLANE = ROWS // PLANES
BLOCKS = ROWS // BQ
LOG2E = 1.4426950408889634


def partner(me, step):
    turn = lax.rem(step, PLANES)
    half = (turn + 1) // 2
    shift = jnp.where(lax.rem(turn, 2) == 1, PLANES // 2 - half, PLANES // 2 + half)
    plane = lax.rem(me // 4 + shift, PLANES)
    lane = lax.rem(step // PLANES + 1, 4)
    mine = lax.rem(me, 4)
    flip_core = lax.rem(lane, 2)
    flip_x = lane // 2
    core = lax.rem(lax.rem(mine, 2) + flip_core, 2)
    x_lo = lax.rem(mine // 2 + flip_x, 2)
    return plane * 4 + x_lo * 2 + core


def arrived(ref, sem):
    pltpu.make_async_copy(ref, ref, sem).wait()


def kernel(
    nbr, query, keys, values, query_tan, keys_tan, values_tan, out, tan,
    kk, vv, qq, oo, own_sem, send_in, recv_kv, recv_q, send_halo, recv_halo, send_out, recv_out,
):
    me = lax.axis_index("heads")
    frame = lax.axis_index("frames")
    plane = me // 4
    nxt = lax.rem(frame + 1, FRAMES)
    prv = lax.rem(frame + FRAMES - 1, FRAMES)

    barrier = pltpu.get_barrier_semaphore()

    def greet(step, carry):
        pl.semaphore_signal(barrier, inc=1, device_id=(partner(me, step), frame), device_id_type=MESH)
        return carry

    lax.fori_loop(0, HEADS - 1, greet, 0)
    for other in (prv, nxt):
        pl.semaphore_signal(barrier, inc=1, device_id=(me, other), device_id_type=MESH)
    pl.semaphore_wait(barrier, HEADS + 1)

    mine = pl.ds(pl.multiple_of(me * TOK, TOK), TOK)
    mine_kv = pl.ds(pl.multiple_of(HALO + me * TOK, TOK), TOK)
    first, second = pl.ds(0, HD), pl.ds(HD, HD)
    moves = (
        (keys, kk.at[mine_kv, first], recv_kv.at[plane]),
        (values, vv.at[mine_kv, first], recv_kv.at[plane]),
        (keys_tan, kk.at[mine_kv, second], recv_kv.at[plane]),
        (values_tan, vv.at[mine_kv, second], recv_kv.at[plane]),
        (query_tan, qq.at[mine, first], recv_q),
        (query, qq.at[mine, second], recv_q),
    )
    for which, (source, target, sem) in enumerate(moves):

        def send(step, carry, which=which, source=source, target=target, sem=sem):
            head = partner(me, step)
            pltpu.make_async_remote_copy(
                src_ref=source.at[:, pl.ds(pl.multiple_of(head * HD, HD), HD)],
                dst_ref=target,
                send_sem=send_in.at[which],
                recv_sem=sem,
                device_id=(head, frame),
                device_id_type=MESH,
            ).start()
            return carry

        lax.fori_loop(0, HEADS - 1, send, 0)
        pltpu.make_async_copy(
            source.at[:, pl.ds(pl.multiple_of(me * HD, HD), HD)], target, own_sem.at[which]
        ).start()
    for which, (source, target, sem) in enumerate(moves):
        arrived(target, own_sem.at[which])

    def plane_wait(index, skip):
        rows = (HEADS // PLANES - skip) * TOK
        arrived(kk.at[pl.ds(0, 2 * rows), :], recv_kv.at[index])

    def planes_wait(indices):
        for index in indices:

            @pl.when(plane == index)
            def _():
                plane_wait(index, 1)

            @pl.when(plane != index)
            def _():
                plane_wait(index, 0)

    sides = (
        ((0, 1), HALO, HALO + ROWS, prv),
        ((PLANES - 2, PLANES - 1), ROWS, 0, nxt),
    )
    copies = []
    for side, (planes, start, landing, other) in enumerate(sides):
        planes_wait(planes)
        for which, buffer in enumerate((kk, vv)):
            copy = pltpu.make_async_remote_copy(
                src_ref=buffer.at[pl.ds(start, HALO), :],
                dst_ref=buffer.at[pl.ds(landing, HALO), :],
                send_sem=send_halo.at[side, which],
                recv_sem=recv_halo.at[side, which],
                device_id=(me, other),
                device_id_type=MESH,
            )
            copy.start()
            copies.append(copy)
    planes_wait(range(2, PLANES - 2))
    arrived(qq.at[pl.ds(0, ROWS - TOK), :], recv_q)
    for copy in copies:
        copy.wait_recv()

    scale = HD**-0.5
    nt = (((1,), (1,)), ((), ()))
    nn = (((1,), (0,)), ((), ()))

    def block_step(step, carry):
        turn = step // 2
        half = (turn + 1) // 2
        shift = jnp.where(lax.rem(turn, 2) == 1, PLANES // 2 - half, PLANES // 2 + half)
        there = lax.rem(plane + shift, PLANES)
        x_lo = lax.rem(lax.rem(me, 4) // 2 + step + 1, 2)
        block = there * 2 + x_lo
        rows = pl.ds(pl.multiple_of(block * BQ, BQ), BQ)
        both = qq[rows, :]
        q = qq[rows, second]
        wins = []
        for slot in range(WK):
            local = jnp.clip(nbr[block, slot] - frame * BLOCKS + HB, 0, BLOCKS + 2 * HB - 1)
            wins.append(pl.ds(local * BQ, BQ))
        scores = [
            lax.dot_general(q, kk[win, first], nt, preferred_element_type=jnp.float32) for win in wins
        ]
        most = functools.reduce(jnp.maximum, [jnp.max(s, axis=1, keepdims=True) for s in scores])
        total = jnp.zeros((BQ, 1), jnp.float32)
        mean = jnp.zeros((BQ, 1), jnp.float32)
        acc = jnp.zeros((BQ, 2 * HD), jnp.float32)
        acc_w = jnp.zeros((BQ, HD), jnp.float32)
        for s, win in zip(scores, wins):
            p = jnp.exp2((s - most) * (scale * LOG2E))
            st = lax.dot_general(both, kk[win, :], nt, preferred_element_type=jnp.float32)
            w = p * st
            total += jnp.sum(p, axis=1, keepdims=True)
            mean += jnp.sum(w, axis=1, keepdims=True)
            v = vv[win, :]
            acc += lax.dot_general(p.astype(jnp.bfloat16), v, nn, preferred_element_type=jnp.float32)
            acc_w += lax.dot_general(
                w.astype(jnp.bfloat16), v[:, :HD], nn, preferred_element_type=jnp.float32
            )
        inv = 1.0 / total
        o = acc[:, :HD] * inv
        t = (acc[:, HD:] + scale * acc_w) * inv - (scale * mean * inv) * o
        oo[0, rows, :] = o.astype(jnp.bfloat16)
        oo[1, rows, :] = t.astype(jnp.bfloat16)
        column = pl.ds(pl.multiple_of(me * HD, HD), HD)
        core = lax.rem(me, 2)
        for flip in (1, 0):
            there_core = lax.rem(core + flip, 2)
            owner = block * 2 + there_core
            piece = pl.ds(pl.multiple_of(owner * TOK, TOK), TOK)
            for which, result in enumerate((out, tan)):

                def remote(which=which, result=result, owner=owner, piece=piece):
                    pltpu.make_async_remote_copy(
                        src_ref=oo.at[which, piece, :],
                        dst_ref=result.at[:, column],
                        send_sem=send_out.at[which],
                        recv_sem=recv_out.at[which],
                        device_id=(owner, frame),
                        device_id_type=MESH,
                    ).start()

                def local(which=which, result=result, piece=piece):
                    pltpu.make_async_copy(
                        oo.at[which, piece, :], result.at[:, column], own_sem.at[which]
                    ).start()

                if flip:
                    remote()
                else:
                    pl.when(step < BLOCKS - 1)(remote)
                    pl.when(step == BLOCKS - 1)(local)
        return carry

    lax.fori_loop(0, BLOCKS, block_step, 0)

    for copy in copies:
        copy.wait_send()
    for which, (source, target, sem) in enumerate(moves):
        arrived(source.at[:, pl.ds(0, (HEADS - 1) * HD)], send_in.at[which])
    for which, result in enumerate((out, tan)):
        rest = result.at[:, pl.ds(0, (HEADS - 1) * HD)]
        arrived(result.at[:, pl.ds(0, HD)], own_sem.at[which])
        arrived(rest, send_out.at[which])
        arrived(rest, recv_out.at[which])


def per_device(query, keys, values, query_tan, keys_tan, values_tan, neighbors):
    shape = jax.ShapeDtypeStruct((TOK, HEADS * HD), jnp.bfloat16)
    hbm = pl.BlockSpec(memory_space=pl.ANY)
    dma = pltpu.SemaphoreType.DMA
    return pl.pallas_call(
        kernel,
        out_shape=(shape, shape),
        in_specs=[pl.BlockSpec(memory_space=pltpu.SMEM)] + [hbm] * 6,
        out_specs=(hbm, hbm),
        scratch_shapes=[
            pltpu.VMEM((ROWS + 2 * HALO, 2 * HD), jnp.bfloat16),
            pltpu.VMEM((ROWS + 2 * HALO, 2 * HD), jnp.bfloat16),
            pltpu.VMEM((ROWS, 2 * HD), jnp.bfloat16),
            pltpu.VMEM((2, ROWS, HD), jnp.bfloat16),
            dma((6,)),
            dma((6,)),
            dma((PLANES,)),
            dma,
            dma((2, 2)),
            dma((2, 2)),
            dma((2,)),
            dma((2,)),
        ],
        compiler_params=pltpu.CompilerParams(
            collective_id=0, has_side_effects=True, vmem_limit_bytes=56 << 20
        ),
        cost_estimate=pl.CostEstimate(
            flops=7 * 10**9, bytes_accessed=20 << 20, transcendentals=5 * 10**6
        ),
        name="attend",
    )(neighbors, query, keys, values, query_tan, keys_tan, values_tan)


def solution(mesh):
    tokens = P(("frames", "heads"), None)
    return jax.shard_map(
        per_device,
        mesh=mesh,
        in_specs=(tokens,) * 6 + (P("frames", None),),
        out_specs=(tokens, tokens),
        check_vma=False,
    )
```

time: 398 us -> 225 us (0.57)
  Pallas kernels: 0 us -> 220 us
  waiting for transfers between devices: 183 us -> 0 us
  matrix products: 59.6 us -> 0 us
  starting transfers between devices: 49.8 us -> 0 us
  local copies, waits for them, and re-layouts: 45.6 us -> 4.71 us
  blocking collectives: 37.3 us -> 0 us
  other arithmetic: 20.2 us -> 0 us
    pallas_call x0 -> x1, Pallas kernels: none -> 220 us  [per_device(): pl.pallas_call(kernel, out_shape=(shape, shape), in_specs=[pl.BlockSpec(m...]
    all_to_all x7 -> x0, waiting for transfers between devices: 143 us -> none  [the longest x1 27.1 us: per_device(): lax.all_to_all(out_h, 'heads', split_axis=0, concat_axis=1, tiled=True)]
    dot_general x5 -> x0, matrix products: 49.3 us -> none  [the longest x1 17.3 us: attend(): jnp.einsum('nqd,nkd->nqk', q_rows, kt_win, preferred_element_type=jnp.flo...]
    all_to_all x7 -> x0, starting transfers between devices: 43.2 us -> none  [the longest x1 11.1 us: per_device(): lax.all_to_all(keys, 'heads', split_axis=1, concat_axis=0, tiled=True)]
    ppermute x2 -> x0, waiting for transfers between devices: 40.4 us -> none  [the longest x1 31.6 us: extended(): after = lax.ppermute(initial, axis, down)]
    all_to_all x1 -> x0, blocking collectives: 37.3 us -> none  [per_device(): lax.all_to_all(tan_h, 'heads', split_axis=0, concat_axis=1, tiled=True)]
    gather x2 -> x0, local copies, waits for them, and re-layouts: 18.8 us -> none  [attend(): chosen = tiles[:, local].reshape(4, blocks, WK * BQ, width)]
    all_to_all x8 -> x0, local copies, waits for them, and re-layouts: 11.3 us -> none  [the longest x1 2.56 us: per_device(): lax.all_to_all(query, 'heads', split_axis=1, concat_axis=0, tiled=True)]
  transfers between devices with their start and end apart: 9 -> 0, of which waited for: 8 -> 0; matrix products, arithmetic and copies ran while one was open for 16% -> 0% of each run, Pallas kernels for 0% -> 0%
where the time goes in v1:
time: 225 us
  Pallas kernels  220 us (98%)
  local copies, waits for them, and re-layouts  4.71 us (2%)
    pallas_call x1, Pallas kernels, per_device(): pl.pallas_call(kernel, out_shape=(shape, shape), in_specs=[pl.BlockSpec(m...  220 us
    unnamed x5, local copies, waits for them, and re-layouts  4.71 us

profile of v1, /device:TPU:1, one launch (start us, length us, event | category | flops | bytes accessed | tf_op | source)
XLA Modules:
  0.0 225.2 jit_solution(6210173072227118178)
XLA Ops:
  0.6 1.4 copy.9.nbr
  2.0 219.8 %attend.1 = (bf16[128,4096]{1,0:T(8,128)(2,1)}, bf16[128,4096]{1,0:T(8,128)(2,1)}) custom-call(s32[16,4]{1,0:T(8,128)} %copy.9.nbr, bf16[128,4096]{1,0:T(8,128)(2,1)} %query.1, bf16[128,4096]{1,0:T(8,128)(2,1)} %keys.1, bf16[128,4096]{1,0:T(8,128)(2,1)} %values.1, bf16[128,4096]{1,0:T(8,128)(2,1)} %query_tan.1, bf16[128,4096]{1,0:T(8,128)(2,1)} %keys_tan.1, ...), custom_call_target="tpu_custom_call" | custom-call | flops 7000000000 | bytes 20971520 | tf_op jit(solution)/shard_map/attend/pallas_call | solution.py:224
  221.8 0.0 copy-start
  221.9 2.4 %copy.12 = bf16[128,4096]{1,0:T(8,128)(2,1)} copy(bf16[128,4096]{1,0:T(8,128)(2,1)} %get-tuple-element.4) | data formatting | bytes 2097152
  224.2 0.0 copy-done
  224.2 1.0 copy.13
Async XLA Ops:
  221.8 2.4 %copy-start = (bf16[128,4096]{1,0:T(8,128)(2,1)S(1)}, bf16[128,4096]{1,0:T(8,128)(2,1)}, u32[]{:S(2)}) copy-start(bf16[128,4096]{1,0:T(8,128)(2,1)} %get-tuple-element.5) | copy-start | bytes 3145732

commit v2 on v1

--- a/solution.py
+++ b/solution.py
@@ -37,19 +37,25 @@
     return plane * 4 + x_lo * 2 + core
 
 
+def head_of(device, frame):
+    x_lo = lax.rem(device // 2, 2)
+    return device + 2 * lax.rem(frame, 2) * (1 - 2 * x_lo)
+
+
 def arrived(ref, sem):
     pltpu.make_async_copy(ref, ref, sem).wait()
 
 
 def kernel(
     nbr, query, keys, values, query_tan, keys_tan, values_tan, out, tan,
-    kk, vv, qq, oo, own_sem, send_in, recv_kv, recv_q, send_halo, recv_halo, send_out, recv_out,
+    kk, vv, qq, oo, send_in, recv_kv, recv_q, send_halo, recv_halo, send_out, recv_out,
 ):
     me = lax.axis_index("heads")
     frame = lax.axis_index("frames")
     plane = me // 4
     nxt = lax.rem(frame + 1, FRAMES)
     prv = lax.rem(frame + FRAMES - 1, FRAMES)
+    beside = me + 2 * (1 - 2 * lax.rem(me // 2, 2))
 
     barrier = pltpu.get_barrier_semaphore()
 
@@ -59,76 +65,86 @@
 
     lax.fori_loop(0, HEADS - 1, greet, 0)
     for other in (prv, nxt):
-        pl.semaphore_signal(barrier, inc=1, device_id=(me, other), device_id_type=MESH)
+        pl.semaphore_signal(barrier, inc=1, device_id=(beside, other), device_id_type=MESH)
     pl.semaphore_wait(barrier, HEADS + 1)
 
     mine = pl.ds(pl.multiple_of(me * TOK, TOK), TOK)
     mine_kv = pl.ds(pl.multiple_of(HALO + me * TOK, TOK), TOK)
     first, second = pl.ds(0, HD), pl.ds(HD, HD)
-    moves = (
-        (keys, kk.at[mine_kv, first], recv_kv.at[plane]),
-        (values, vv.at[mine_kv, first], recv_kv.at[plane]),
-        (keys_tan, kk.at[mine_kv, second], recv_kv.at[plane]),
-        (values_tan, vv.at[mine_kv, second], recv_kv.at[plane]),
-        (query_tan, qq.at[mine, first], recv_q),
-        (query, qq.at[mine, second], recv_q),
-    )
-    for which, (source, target, sem) in enumerate(moves):
-
-        def send(step, carry, which=which, source=source, target=target, sem=sem):
-            head = partner(me, step)
+    group = (plane + 2) // 4
+    window = ((keys, kk, first), (values, vv, first), (keys_tan, kk, second), (values_tan, vv, second))
+    queries = ((query_tan, first), (query, second))
+
+    def column(device):
+        return pl.ds(pl.multiple_of(head_of(device, frame) * HD, HD), HD)
+
+    def send_window(which):
+        source, buffer, part = window[which]
+        target, sem = buffer.at[mine_kv, part], recv_kv.at[which, group]
+
+        def send(step, carry):
+            there = partner(me, step)
             pltpu.make_async_remote_copy(
-                src_ref=source.at[:, pl.ds(pl.multiple_of(head * HD, HD), HD)],
+                src_ref=source.at[:, column(there)],
                 dst_ref=target,
                 send_sem=send_in.at[which],
                 recv_sem=sem,
-                device_id=(head, frame),
+                device_id=(there, frame),
                 device_id_type=MESH,
             ).start()
             return carry
 
         lax.fori_loop(0, HEADS - 1, send, 0)
-        pltpu.make_async_copy(
-            source.at[:, pl.ds(pl.multiple_of(me * HD, HD), HD)], target, own_sem.at[which]
-        ).start()
-    for which, (source, target, sem) in enumerate(moves):
-        arrived(target, own_sem.at[which])
-
-    def plane_wait(index, skip):
-        rows = (HEADS // PLANES - skip) * TOK
-        arrived(kk.at[pl.ds(0, 2 * rows), :], recv_kv.at[index])
-
-    def planes_wait(indices):
-        for index in indices:
-
-            @pl.when(plane == index)
-            def _():
-                plane_wait(index, 1)
-
-            @pl.when(plane != index)
-            def _():
-                plane_wait(index, 0)
-
-    sides = (
-        ((0, 1), HALO, HALO + ROWS, prv),
-        ((PLANES - 2, PLANES - 1), ROWS, 0, nxt),
-    )
+        pltpu.make_async_copy(source.at[:, column(me)], target, sem).start()
+
+    def send_queries(start, stop):
+        def send(step, carry):
+            there = partner(me, lax.rem(step, 4) * PLANES + step // 4)
+            for which, (source, part) in enumerate(queries):
+                pltpu.make_async_remote_copy(
+                    src_ref=source.at[:, column(there)],
+                    dst_ref=qq.at[mine, part],
+                    send_sem=send_in.at[4 + which],
+                    recv_sem=recv_q.at[plane],
+                    device_id=(there, frame),
+                    device_id_type=MESH,
+                ).start()
+            return carry
+
+        lax.fori_loop(start, stop, send, 0)
+
     copies = []
-    for side, (planes, start, landing, other) in enumerate(sides):
-        planes_wait(planes)
-        for which, buffer in enumerate((kk, vv)):
+
+    def forward(which):
+        buffer, part = window[which][1:]
+        sides = ((0, HALO, HALO + ROWS, prv), (2, ROWS, 0, nxt))
+        for side, (edge, start, landing, other) in enumerate(sides):
+            arrived(buffer.at[pl.ds(start, HALO), part], recv_kv.at[which, edge])
             copy = pltpu.make_async_remote_copy(
-                src_ref=buffer.at[pl.ds(start, HALO), :],
-                dst_ref=buffer.at[pl.ds(landing, HALO), :],
-                send_sem=send_halo.at[side, which],
-                recv_sem=recv_halo.at[side, which],
-                device_id=(me, other),
+                src_ref=buffer.at[pl.ds(start, HALO), part],
+                dst_ref=buffer.at[pl.ds(landing, HALO), part],
+                send_sem=send_halo.at[which, side],
+                recv_sem=recv_halo.at[which, side],
+                device_id=(beside, other),
                 device_id_type=MESH,
             )
             copy.start()
             copies.append(copy)
-    planes_wait(range(2, PLANES - 2))
-    arrived(qq.at[pl.ds(0, ROWS - TOK), :], recv_q)
+
+    send_window(0)
+    send_window(1)
+    forward(0)
+    send_window(2)
+    forward(1)
+    send_window(3)
+    forward(2)
+    send_queries(0, 12)
+    forward(3)
+    send_queries(12, HEADS - 1)
+    for which, (source, part) in enumerate(queries):
+        pltpu.make_async_copy(source.at[:, column(me)], qq.at[mine, part], recv_q.at[plane]).start()
+    for which, (source, buffer, part) in enumerate(window):
+        arrived(buffer.at[pl.ds(HALO + 2 * PLANE, 4 * PLANE), part], recv_kv.at[which, 1])
     for copy in copies:
         copy.wait_recv()
 
@@ -144,11 +160,16 @@
         x_lo = lax.rem(lax.rem(me, 4) // 2 + step + 1, 2)
         block = there * 2 + x_lo
         rows = pl.ds(pl.multiple_of(block * BQ, BQ), BQ)
+
+        @pl.when(lax.rem(step, 2) == 0)
+        def _():
+            arrived(qq.at[pl.ds(pl.multiple_of(there * PLANE, PLANE), PLANE), :], recv_q.at[there])
+
         both = qq[rows, :]
         q = qq[rows, second]
         wins = []
         for slot in range(WK):
-            local = jnp.clip(nbr[block, slot] - frame * BLOCKS + HB, 0, BLOCKS + 2 * HB - 1)
+            local = jnp.clip(nbr[slot, block] - frame * BLOCKS + HB, 0, BLOCKS + 2 * HB - 1)
             wins.append(pl.ds(local * BQ, BQ))
         scores = [
             lax.dot_general(q, kk[win, first], nt, preferred_element_type=jnp.float32) for win in wins
@@ -174,7 +195,7 @@
         t = (acc[:, HD:] + scale * acc_w) * inv - (scale * mean * inv) * o
         oo[0, rows, :] = o.astype(jnp.bfloat16)
         oo[1, rows, :] = t.astype(jnp.bfloat16)
-        column = pl.ds(pl.multiple_of(me * HD, HD), HD)
+        home = column(me)
         core = lax.rem(me, 2)
         for flip in (1, 0):
             there_core = lax.rem(core + flip, 2)
@@ -185,7 +206,7 @@
                 def remote(which=which, result=result, owner=owner, piece=piece):
                     pltpu.make_async_remote_copy(
                         src_ref=oo.at[which, piece, :],
-                        dst_ref=result.at[:, column],
+                        dst_ref=result.at[:, home],
                         send_sem=send_out.at[which],
                         recv_sem=recv_out.at[which],
                         device_id=(owner, frame),
@@ -194,7 +215,7 @@
 
                 def local(which=which, result=result, piece=piece):
                     pltpu.make_async_copy(
-                        oo.at[which, piece, :], result.at[:, column], own_sem.at[which]
+                        oo.at[which, piece, :], result.at[:, home], recv_out.at[which]
                     ).start()
 
                 if flip:
@@ -208,13 +229,12 @@
 
     for copy in copies:
         copy.wait_send()
-    for which, (source, target, sem) in enumerate(moves):
-        arrived(source.at[:, pl.ds(0, (HEADS - 1) * HD)], send_in.at[which])
+    rest = pl.ds(0, (HEADS - 1) * HD)
+    for which in range(6):
+        arrived(out.at[:, rest], send_in.at[which])
     for which, result in enumerate((out, tan)):
-        rest = result.at[:, pl.ds(0, (HEADS - 1) * HD)]
-        arrived(result.at[:, pl.ds(0, HD)], own_sem.at[which])
-        arrived(rest, send_out.at[which])
-        arrived(rest, recv_out.at[which])
+        arrived(result.at[:, rest], send_out.at[which])
+        arrived(result, recv_out.at[which])
 
 
 def per_device(query, keys, values, query_tan, keys_tan, values_tan, neighbors):
@@ -232,11 +252,10 @@
             pltpu.VMEM((ROWS, 2 * HD), jnp.bfloat16),
             pltpu.VMEM((2, ROWS, HD), jnp.bfloat16),
             dma((6,)),
-            dma((6,)),
+            dma((4, 3)),
             dma((PLANES,)),
-            dma,
-            dma((2, 2)),
-            dma((2, 2)),
+            dma((4, 2)),
+            dma((4, 2)),
             dma((2,)),
             dma((2,)),
         ],
@@ -247,7 +266,7 @@
             flops=7 * 10**9, bytes_accessed=20 << 20, transcendentals=5 * 10**6
         ),
         name="attend",
-    )(neighbors, query, keys, values, query_tan, keys_tan, values_tan)
+    )(neighbors.T, query, keys, values, query_tan, keys_tan, values_tan)
 
 
 def solution(mesh):

time: 225 us -> 199 us (0.88)
  Pallas kernels: 220 us -> 195 us
    pallas_call x1, Pallas kernels: 220 us -> 195 us  [per_device(): pl.pallas_call(kernel, out_shape=(shape, shape), in_specs=[pl.BlockSpec(m...]
    unnamed x5 -> x4, local copies, waits for them, and re-layouts: 4.71 us -> 3.35 us
where the time goes in v2:
time: 199 us
  Pallas kernels  195 us (98%)
  local copies, waits for them, and re-layouts  3.35 us (2%)
    pallas_call x1, Pallas kernels, per_device(): pl.pallas_call(kernel, out_shape=(shape, shape), in_specs=[pl.BlockSpec(m...  195 us

profile of v2, /device:TPU:1, one launch (start us, length us, event | category | flops | bytes accessed | tf_op | source)
XLA Modules:
  0.0 198.7 jit_solution(14149886456912515758)
XLA Ops:
  0.6 194.7 %attend.1 = (bf16[128,4096]{1,0:T(8,128)(2,1)}, bf16[128,4096]{1,0:T(8,128)(2,1)}) custom-call(s32[4,16]{1,0:T(4,128)} %bitcast.1, bf16[128,4096]{1,0:T(8,128)(2,1)} %query.1, bf16[128,4096]{1,0:T(8,128)(2,1)} %keys.1, bf16[128,4096]{1,0:T(8,128)(2,1)} %values.1, bf16[128,4096]{1,0:T(8,128)(2,1)} %query_tan.1, bf16[128,4096]{1,0:T(8,128)(2,1)} %keys_tan.1, ...), custom_call_target="tpu_custom_call" | custom-call | flops 7000000000 | bytes 20971520 | tf_op jit(solution)/shard_map/attend/pallas_call | solution.py:244
  195.4 0.0 copy-start
  195.4 2.4 %copy.11 = bf16[128,4096]{1,0:T(8,128)(2,1)} copy(bf16[128,4096]{1,0:T(8,128)(2,1)} %get-tuple-element.4) | data formatting | bytes 2097152
  197.8 0.0 copy-done
  197.8 1.0 copy.12
Async XLA Ops:
  195.4 2.4 %copy-start = (bf16[128,4096]{1,0:T(8,128)(2,1)S(1)}, bf16[128,4096]{1,0:T(8,128)(2,1)}, u32[]{:S(2)}) copy-start(bf16[128,4096]{1,0:T(8,128)(2,1)} %get-tuple-element.5) | copy-start | bytes 3145732

commit v3 on v2

--- a/solution.py
+++ b/solution.py
@@ -59,11 +59,12 @@
 
     barrier = pltpu.get_barrier_semaphore()
 
-    def greet(step, carry):
-        pl.semaphore_signal(barrier, inc=1, device_id=(partner(me, step), frame), device_id_type=MESH)
-        return carry
-
-    lax.fori_loop(0, HEADS - 1, greet, 0)
+    mates = [lax.rem(me, 4), beside - 4 * plane]
+    mates = mates + [mate + 1 - 2 * lax.rem(mate, 2) for mate in mates]
+    for shift in (4, 3, 5, 2, 6, 1, 7, 0):
+        there = lax.rem(plane + shift, PLANES) * 4
+        for mate in mates[1:] if shift == 0 else mates:
+            pl.semaphore_signal(barrier, inc=1, device_id=(there + mate, frame), device_id_type=MESH)
     for other in (prv, nxt):
         pl.semaphore_signal(barrier, inc=1, device_id=(beside, other), device_id_type=MESH)
     pl.semaphore_wait(barrier, HEADS + 1)
@@ -243,7 +244,7 @@
     dma = pltpu.SemaphoreType.DMA
     return pl.pallas_call(
         kernel,
-        out_shape=(shape, shape),
+        out_shape=(pltpu.VMEM((TOK, HEADS * HD), jnp.bfloat16),) * 2,
         in_specs=[pl.BlockSpec(memory_space=pltpu.SMEM)] + [hbm] * 6,
         out_specs=(hbm, hbm),
         scratch_shapes=[

time: 199 us -> 197 us (0.990)
  no operation moved by 1% of the time
where the time goes in v3:
time: 197 us; the launch traced here: 196 us
  Pallas kernels  194 us (98%)
    pallas_call x1, Pallas kernels, per_device(): pl.pallas_call(kernel, out_shape=(pltpu.VMEM((TOK, HEADS * HD), jnp.bfloa...  194 us

profile of v3, /device:TPU:1, one launch (start us, length us, event | category | flops | bytes accessed | tf_op | source)
XLA Modules:
  0.0 196.1 jit_solution(16980663771055629385)
XLA Ops:
  0.6 193.6 %attend.1 = (bf16[128,4096]{1,0:T(8,128)(2,1)S(1)}, bf16[128,4096]{1,0:T(8,128)(2,1)S(1)}) custom-call(s32[4,16]{1,0:T(4,128)} %bitcast.1, bf16[128,4096]{1,0:T(8,128)(2,1)} %query.1, bf16[128,4096]{1,0:T(8,128)(2,1)} %keys.1, bf16[128,4096]{1,0:T(8,128)(2,1)} %values.1, bf16[128,4096]{1,0:T(8,128)(2,1)} %query_tan.1, bf16[128,4096]{1,0:T(8,128)(2,1)} %keys_tan.1, ...), custom_call_target="tpu_custom_call" | custom-call | flops 7000000000 | bytes 20971520 | tf_op jit(solution)/shard_map/attend/pallas_call | solution.py:245
  194.2 1.0 copy.11
  195.2 1.0 copy.12

commit v4 on v3

--- a/solution.py
+++ b/solution.py
@@ -47,8 +47,8 @@
 
 
 def kernel(
-    nbr, query, keys, values, query_tan, keys_tan, values_tan, out, tan,
-    kk, vv, qq, oo, send_in, recv_kv, recv_q, send_halo, recv_halo, send_out, recv_out,
+    table, query, keys, values, query_tan, keys_tan, values_tan, out, tan,
+    nbr, kk, vv, qq, oo, table_sem, send_in, recv_kv, recv_q, send_halo, recv_halo, send_out, recv_out,
 ):
     me = lax.axis_index("heads")
     frame = lax.axis_index("frames")
@@ -67,6 +67,8 @@
             pl.semaphore_signal(barrier, inc=1, device_id=(there + mate, frame), device_id_type=MESH)
     for other in (prv, nxt):
         pl.semaphore_signal(barrier, inc=1, device_id=(beside, other), device_id_type=MESH)
+    fetch = pltpu.make_async_copy(table, nbr, table_sem)
+    fetch.start()
     pl.semaphore_wait(barrier, HEADS + 1)
 
     mine = pl.ds(pl.multiple_of(me * TOK, TOK), TOK)
@@ -148,6 +150,7 @@
         arrived(buffer.at[pl.ds(HALO + 2 * PLANE, 4 * PLANE), part], recv_kv.at[which, 1])
     for copy in copies:
         copy.wait_recv()
+    fetch.wait()
 
     scale = HD**-0.5
     nt = (((1,), (1,)), ((), ()))
@@ -245,13 +248,15 @@
     return pl.pallas_call(
         kernel,
         out_shape=(pltpu.VMEM((TOK, HEADS * HD), jnp.bfloat16),) * 2,
-        in_specs=[pl.BlockSpec(memory_space=pltpu.SMEM)] + [hbm] * 6,
+        in_specs=[hbm] * 7,
         out_specs=(hbm, hbm),
         scratch_shapes=[
+            pltpu.SMEM((WK, BLOCKS), jnp.int32),
             pltpu.VMEM((ROWS + 2 * HALO, 2 * HD), jnp.bfloat16),
             pltpu.VMEM((ROWS + 2 * HALO, 2 * HD), jnp.bfloat16),
             pltpu.VMEM((ROWS, 2 * HD), jnp.bfloat16),
             pltpu.VMEM((2, ROWS, HD), jnp.bfloat16),
+            dma,
             dma((6,)),
             dma((4, 3)),
             dma((PLANES,)),

time: 197 us -> 196 us (level)
  no operation moved by 1% of the time
where the time goes in v4:
time: 196 us; the launch traced here: 195 us
  Pallas kernels  193 us (98%)
    pallas_call x1, Pallas kernels, per_device(): pl.pallas_call(kernel, out_shape=(pltpu.VMEM((TOK, HEADS * HD), jnp.bfloa...  193 us

profile of v4, /device:TPU:1, one launch (start us, length us, event | category | flops | bytes accessed | tf_op | source)
XLA Modules:
  0.0 195.5 jit_solution(10138515620253091259)
XLA Ops:
  0.6 192.9 %attend.1 = (bf16[128,4096]{1,0:T(8,128)(2,1)S(1)}, bf16[128,4096]{1,0:T(8,128)(2,1)S(1)}) custom-call(s32[4,16]{1,0:T(4,128)} %bitcast.1, bf16[128,4096]{1,0:T(8,128)(2,1)} %query.1, bf16[128,4096]{1,0:T(8,128)(2,1)} %keys.1, bf16[128,4096]{1,0:T(8,128)(2,1)} %values.1, bf16[128,4096]{1,0:T(8,128)(2,1)} %query_tan.1, bf16[128,4096]{1,0:T(8,128)(2,1)} %keys_tan.1, ...), custom_call_target="tpu_custom_call" | custom-call | flops 7000000000 | bytes 20971520 | tf_op jit(solution)/shard_map/attend/pallas_call | solution.py:248
  193.5 1.0 copy.11
  194.5 1.0 copy.12

commit v5 on v4

--- a/solution.py
+++ b/solution.py
@@ -48,7 +48,7 @@
 
 def kernel(
     table, query, keys, values, query_tan, keys_tan, values_tan, out, tan,
-    nbr, kk, vv, qq, oo, table_sem, send_in, recv_kv, recv_q, send_halo, recv_halo, send_out, recv_out,
+    nbr, kk, vv, qq, oo, ready, table_sem, send_in, recv_kv, recv_q, send_halo, recv_halo, send_out, recv_out,
 ):
     me = lax.axis_index("heads")
     frame = lax.axis_index("frames")
@@ -59,17 +59,21 @@
 
     barrier = pltpu.get_barrier_semaphore()
 
-    mates = [lax.rem(me, 4), beside - 4 * plane]
-    mates = mates + [mate + 1 - 2 * lax.rem(mate, 2) for mate in mates]
-    for shift in (4, 3, 5, 2, 6, 1, 7, 0):
-        there = lax.rem(plane + shift, PLANES) * 4
-        for mate in mates[1:] if shift == 0 else mates:
-            pl.semaphore_signal(barrier, inc=1, device_id=(there + mate, frame), device_id_type=MESH)
+    lane = lax.rem(me, 4)
+    flip = lane + 1 - 2 * lax.rem(lane, 2)
+    mates = [flip + 4 * plane, beside, beside + flip - lane]
+    for shift in (4, 3, 5, 2, 6, 1, 7):
+        there = lax.rem(plane + shift, PLANES) * 4 + lane
+        pl.semaphore_signal(barrier, inc=1, device_id=(there, frame), device_id_type=MESH)
+    for mate in mates:
+        pl.semaphore_signal(barrier, inc=1, device_id=(mate, frame), device_id_type=MESH)
     for other in (prv, nxt):
         pl.semaphore_signal(barrier, inc=1, device_id=(beside, other), device_id_type=MESH)
     fetch = pltpu.make_async_copy(table, nbr, table_sem)
     fetch.start()
-    pl.semaphore_wait(barrier, HEADS + 1)
+    pl.semaphore_wait(barrier, PLANES - 1 + len(mates) + 2)
+    for mate in mates:
+        pl.semaphore_signal(ready, inc=1, device_id=(mate, frame), device_id_type=MESH)
 
     mine = pl.ds(pl.multiple_of(me * TOK, TOK), TOK)
     mine_kv = pl.ds(pl.multiple_of(HALO + me * TOK, TOK), TOK)
@@ -97,7 +101,12 @@
             ).start()
             return carry
 
-        lax.fori_loop(0, HEADS - 1, send, 0)
+        if which == 0:
+            lax.fori_loop(HEADS - PLANES, HEADS - 1, send, 0)
+            pl.semaphore_wait(ready, len(mates))
+            lax.fori_loop(0, HEADS - PLANES, send, 0)
+        else:
+            lax.fori_loop(0, HEADS - 1, send, 0)
         pltpu.make_async_copy(source.at[:, column(me)], target, sem).start()
 
     def send_queries(start, stop):
@@ -241,11 +250,22 @@
         arrived(result, recv_out.at[which])
 
 
+def hand_on(out, tan, out_copy, tan_copy, sems):
+    copies = [
+        pltpu.make_async_copy(out, out_copy, sems.at[0]),
+        pltpu.make_async_copy(tan, tan_copy, sems.at[1]),
+    ]
+    for copy in copies:
+        copy.start()
+    for copy in copies:
+        copy.wait()
+
+
 def per_device(query, keys, values, query_tan, keys_tan, values_tan, neighbors):
     shape = jax.ShapeDtypeStruct((TOK, HEADS * HD), jnp.bfloat16)
     hbm = pl.BlockSpec(memory_space=pl.ANY)
     dma = pltpu.SemaphoreType.DMA
-    return pl.pallas_call(
+    results = pl.pallas_call(
         kernel,
         out_shape=(pltpu.VMEM((TOK, HEADS * HD), jnp.bfloat16),) * 2,
         in_specs=[hbm] * 7,
@@ -256,6 +276,7 @@
             pltpu.VMEM((ROWS + 2 * HALO, 2 * HD), jnp.bfloat16),
             pltpu.VMEM((ROWS, 2 * HD), jnp.bfloat16),
             pltpu.VMEM((2, ROWS, HD), jnp.bfloat16),
+            pltpu.SemaphoreType.REGULAR,
             dma,
             dma((6,)),
             dma((4, 3)),
@@ -273,6 +294,15 @@
         ),
         name="attend",
     )(neighbors.T, query, keys, values, query_tan, keys_tan, values_tan)
+    results = [pltpu.with_memory_space_constraint(result, pltpu.VMEM) for result in results]
+    return pl.pallas_call(
+        hand_on,
+        out_shape=(shape, shape),
+        in_specs=[pl.BlockSpec(memory_space=pltpu.VMEM)] * 2,
+        out_specs=(hbm, hbm),
+        scratch_shapes=[dma((2,))],
+        name="hand_on",
+    )(*results)
 
 
 def solution(mesh):

time: 196 us -> 195 us (level)
  no operation moved by 1% of the time
where the time goes in v5:
time: 195 us
  Pallas kernels  194 us (99%)
    pallas_call x1, Pallas kernels, per_device(): pl.pallas_call(kernel, out_shape=(pltpu.VMEM((TOK, HEADS * HD), jnp.bfloa...  193 us

profile of v5, /device:TPU:1, one launch (start us, length us, event | category | flops | bytes accessed | tf_op | source)
XLA Modules:
  0.0 194.7 jit_solution(12961960910011698588)
XLA Ops:
  0.6 192.8 %attend.1 = (bf16[128,4096]{1,0:T(8,128)(2,1)S(1)}, bf16[128,4096]{1,0:T(8,128)(2,1)S(1)}) custom-call(s32[4,16]{1,0:T(4,128)} %bitcast.1, bf16[128,4096]{1,0:T(8,128)(2,1)} %query.1, bf16[128,4096]{1,0:T(8,128)(2,1)} %keys.1, bf16[128,4096]{1,0:T(8,128)(2,1)} %values.1, bf16[128,4096]{1,0:T(8,128)(2,1)} %query_tan.1, bf16[128,4096]{1,0:T(8,128)(2,1)} %keys_tan.1, ...), custom_call_target="tpu_custom_call" | custom-call | flops 7000000000 | bytes 20971520 | tf_op jit(solution)/shard_map/attend/pallas_call | solution.py:268
  193.4 1.3 hand_on.1

commit v6 on v5

--- a/solution.py
+++ b/solution.py
@@ -68,10 +68,11 @@
     for mate in mates:
         pl.semaphore_signal(barrier, inc=1, device_id=(mate, frame), device_id_type=MESH)
     for other in (prv, nxt):
-        pl.semaphore_signal(barrier, inc=1, device_id=(beside, other), device_id_type=MESH)
+        pl.semaphore_signal(barrier, inc=1, device_id=(4 * plane + 3, other), device_id_type=MESH)
     fetch = pltpu.make_async_copy(table, nbr, table_sem)
     fetch.start()
-    pl.semaphore_wait(barrier, PLANES - 1 + len(mates) + 2)
+    known = PLANES - 1 + len(mates)
+    pl.semaphore_wait(barrier, jnp.where(lane == 3, known + 2 * 4, known))
     for mate in mates:
         pl.semaphore_signal(ready, inc=1, device_id=(mate, frame), device_id_type=MESH)
 

time: 195 us -> 194 us (level)
  no operation moved by 1% of the time
where the time goes in v6:
time: 194 us
  Pallas kernels  193 us (99%)
    pallas_call x1, Pallas kernels, per_device(): pl.pallas_call(kernel, out_shape=(pltpu.VMEM((TOK, HEADS * HD), jnp.bfloa...  192 us

profile of v6, /device:TPU:1, one launch (start us, length us, event | category | flops | bytes accessed | tf_op | source)
XLA Modules:
  0.0 193.6 jit_solution(3037914978398363417)
XLA Ops:
  0.6 191.7 %attend.1 = (bf16[128,4096]{1,0:T(8,128)(2,1)S(1)}, bf16[128,4096]{1,0:T(8,128)(2,1)S(1)}) custom-call(s32[4,16]{1,0:T(4,128)} %bitcast.1, bf16[128,4096]{1,0:T(8,128)(2,1)} %query.1, bf16[128,4096]{1,0:T(8,128)(2,1)} %keys.1, bf16[128,4096]{1,0:T(8,128)(2,1)} %values.1, bf16[128,4096]{1,0:T(8,128)(2,1)} %query_tan.1, bf16[128,4096]{1,0:T(8,128)(2,1)} %keys_tan.1, ...), custom_call_target="tpu_custom_call" | custom-call | flops 7000000000 | bytes 20971520 | tf_op jit(solution)/shard_map/attend/pallas_call | solution.py:269
  192.3 1.3 hand_on.1

commit v7 on v6

--- a/solution.py
+++ b/solution.py
@@ -189,24 +189,23 @@
             lax.dot_general(q, kk[win, first], nt, preferred_element_type=jnp.float32) for win in wins
         ]
         most = functools.reduce(jnp.maximum, [jnp.max(s, axis=1, keepdims=True) for s in scores])
-        total = jnp.zeros((BQ, 1), jnp.float32)
+        weights = [jnp.exp2((s - most) * (scale * LOG2E)) for s in scores]
+        inv = 1.0 / functools.reduce(jnp.add, [jnp.sum(p, axis=1, keepdims=True) for p in weights])
         mean = jnp.zeros((BQ, 1), jnp.float32)
         acc = jnp.zeros((BQ, 2 * HD), jnp.float32)
         acc_w = jnp.zeros((BQ, HD), jnp.float32)
-        for s, win in zip(scores, wins):
-            p = jnp.exp2((s - most) * (scale * LOG2E))
+        for p, win in zip(weights, wins):
+            p = p * inv
             st = lax.dot_general(both, kk[win, :], nt, preferred_element_type=jnp.float32)
-            w = p * st
-            total += jnp.sum(p, axis=1, keepdims=True)
+            w = p * (st * scale)
             mean += jnp.sum(w, axis=1, keepdims=True)
             v = vv[win, :]
             acc += lax.dot_general(p.astype(jnp.bfloat16), v, nn, preferred_element_type=jnp.float32)
             acc_w += lax.dot_general(
                 w.astype(jnp.bfloat16), v[:, :HD], nn, preferred_element_type=jnp.float32
             )
-        inv = 1.0 / total
-        o = acc[:, :HD] * inv
-        t = (acc[:, HD:] + scale * acc_w) * inv - (scale * mean * inv) * o
+        o = acc[:, :HD]
+        t = acc[:, HD:] + acc_w - mean * o
         oo[0, rows, :] = o.astype(jnp.bfloat16)
         oo[1, rows, :] = t.astype(jnp.bfloat16)
         home = column(me)

time: 194 us -> 194 us (level)
  no operation moved by 1% of the time
where the time goes in v7:
time: 194 us
  Pallas kernels  193 us (99%)
    pallas_call x1, Pallas kernels, per_device(): pl.pallas_call(kernel, out_shape=(pltpu.VMEM((TOK, HEADS * HD), jnp.bfloa...  192 us

profile of v7, /device:TPU:1, one launch (start us, length us, event | category | flops | bytes accessed | tf_op | source)
XLA Modules:
  0.0 193.6 jit_solution(4535426335259453622)
XLA Ops:
  0.6 191.7 %attend.1 = (bf16[128,4096]{1,0:T(8,128)(2,1)S(1)}, bf16[128,4096]{1,0:T(8,128)(2,1)S(1)}) custom-call(s32[4,16]{1,0:T(4,128)} %bitcast.1, bf16[128,4096]{1,0:T(8,128)(2,1)} %query.1, bf16[128,4096]{1,0:T(8,128)(2,1)} %keys.1, bf16[128,4096]{1,0:T(8,128)(2,1)} %values.1, bf16[128,4096]{1,0:T(8,128)(2,1)} %query_tan.1, bf16[128,4096]{1,0:T(8,128)(2,1)} %keys_tan.1, ...), custom_call_target="tpu_custom_call" | custom-call | flops 7000000000 | bytes 20971520 | tf_op jit(solution)/shard_map/attend/pallas_call | solution.py:268
  192.3 1.3 hand_on.1

commit v8 on v7

--- a/solution.py
+++ b/solution.py
@@ -110,21 +110,22 @@
             lax.fori_loop(0, HEADS - 1, send, 0)
         pltpu.make_async_copy(source.at[:, column(me)], target, sem).start()
 
-    def send_queries(start, stop):
+    def send_queries(which):
+        source, part = queries[which]
+
         def send(step, carry):
             there = partner(me, lax.rem(step, 4) * PLANES + step // 4)
-            for which, (source, part) in enumerate(queries):
-                pltpu.make_async_remote_copy(
-                    src_ref=source.at[:, column(there)],
-                    dst_ref=qq.at[mine, part],
-                    send_sem=send_in.at[4 + which],
-                    recv_sem=recv_q.at[plane],
-                    device_id=(there, frame),
-                    device_id_type=MESH,
-                ).start()
+            pltpu.make_async_remote_copy(
+                src_ref=source.at[:, column(there)],
+                dst_ref=qq.at[mine, part],
+                send_sem=send_in.at[4 + which],
+                recv_sem=recv_q.at[plane],
+                device_id=(there, frame),
+                device_id_type=MESH,
+            ).start()
             return carry
 
-        lax.fori_loop(start, stop, send, 0)
+        lax.fori_loop(0, HEADS - 1, send, 0)
 
     copies = []
 
@@ -151,9 +152,9 @@
     forward(1)
     send_window(3)
     forward(2)
-    send_queries(0, 12)
+    send_queries(0)
     forward(3)
-    send_queries(12, HEADS - 1)
+    send_queries(1)
     for which, (source, part) in enumerate(queries):
         pltpu.make_async_copy(source.at[:, column(me)], qq.at[mine, part], recv_q.at[plane]).start()
     for which, (source, buffer, part) in enumerate(window):

time: 194 us -> 193 us (level)
  no operation moved by 1% of the time
where the time goes in v8:
time: 193 us; the launch traced here: 192 us
  Pallas kernels  192 us (99%)
    pallas_call x1, Pallas kernels, per_device(): pl.pallas_call(kernel, out_shape=(pltpu.VMEM((TOK, HEADS * HD), jnp.bfloa...  190 us

profile of v8, /device:TPU:1, one launch (start us, length us, event | category | flops | bytes accessed | tf_op | source)
XLA Modules:
  0.0 192.3 jit_solution(11053042348981855173)
XLA Ops:
  0.6 190.4 %attend.1 = (bf16[128,4096]{1,0:T(8,128)(2,1)S(1)}, bf16[128,4096]{1,0:T(8,128)(2,1)S(1)}) custom-call(s32[4,16]{1,0:T(4,128)} %bitcast.1, bf16[128,4096]{1,0:T(8,128)(2,1)} %query.1, bf16[128,4096]{1,0:T(8,128)(2,1)} %keys.1, bf16[128,4096]{1,0:T(8,128)(2,1)} %values.1, bf16[128,4096]{1,0:T(8,128)(2,1)} %query_tan.1, bf16[128,4096]{1,0:T(8,128)(2,1)} %keys_tan.1, ...), custom_call_target="tpu_custom_call" | custom-call | flops 7000000000 | bytes 20971520 | tf_op jit(solution)/shard_map/attend/pallas_call | solution.py:269
  191.0 1.3 hand_on.1

commit v9 on v8

--- a/solution.py
+++ b/solution.py
@@ -167,13 +167,45 @@
     nt = (((1,), (1,)), ((), ()))
     nn = (((1,), (0,)), ((), ()))
 
-    def block_step(step, carry):
+    def block_of(step):
         turn = step // 2
         half = (turn + 1) // 2
         shift = jnp.where(lax.rem(turn, 2) == 1, PLANES // 2 - half, PLANES // 2 + half)
         there = lax.rem(plane + shift, PLANES)
         x_lo = lax.rem(lax.rem(me, 4) // 2 + step + 1, 2)
         block = there * 2 + x_lo
+        return there, block
+
+    def send_back(step, block, which):
+        result = (out, tan)[which]
+        home = column(me)
+        for flip in (1, 0):
+            owner = block * 2 + lax.rem(me + flip, 2)
+            piece = pl.ds(pl.multiple_of(owner * TOK, TOK), TOK)
+
+            def remote(owner=owner, piece=piece):
+                pltpu.make_async_remote_copy(
+                    src_ref=oo.at[which, piece, :],
+                    dst_ref=result.at[:, home],
+                    send_sem=send_out.at[which],
+                    recv_sem=recv_out.at[which],
+                    device_id=(owner, frame),
+                    device_id_type=MESH,
+                ).start()
+
+            def local(piece=piece):
+                pltpu.make_async_copy(
+                    oo.at[which, piece, :], result.at[:, home], recv_out.at[which]
+                ).start()
+
+            if flip:
+                remote()
+            else:
+                pl.when(step < BLOCKS - 1)(remote)
+                pl.when(step == BLOCKS - 1)(local)
+
+    def block_step(step, carry):
+        there, block = block_of(step)
         rows = pl.ds(pl.multiple_of(block * BQ, BQ), BQ)
 
         @pl.when(lax.rem(step, 2) == 0)
@@ -209,37 +241,15 @@
         t = acc[:, HD:] + acc_w - mean * o
         oo[0, rows, :] = o.astype(jnp.bfloat16)
         oo[1, rows, :] = t.astype(jnp.bfloat16)
-        home = column(me)
-        core = lax.rem(me, 2)
-        for flip in (1, 0):
-            there_core = lax.rem(core + flip, 2)
-            owner = block * 2 + there_core
-            piece = pl.ds(pl.multiple_of(owner * TOK, TOK), TOK)
-            for which, result in enumerate((out, tan)):
-
-                def remote(which=which, result=result, owner=owner, piece=piece):
-                    pltpu.make_async_remote_copy(
-                        src_ref=oo.at[which, piece, :],
-                        dst_ref=result.at[:, home],
-                        send_sem=send_out.at[which],
-                        recv_sem=recv_out.at[which],
-                        device_id=(owner, frame),
-                        device_id_type=MESH,
-                    ).start()
-
-                def local(which=which, result=result, piece=piece):
-                    pltpu.make_async_copy(
-                        oo.at[which, piece, :], result.at[:, home], recv_out.at[which]
-                    ).start()
-
-                if flip:
-                    remote()
-                else:
-                    pl.when(step < BLOCKS - 1)(remote)
-                    pl.when(step == BLOCKS - 1)(local)
+        send_back(step, block, 0)
         return carry
 
+    def tan_step(step, carry):
+        send_back(step, block_of(step)[1], 1)
+        return carry
+
     lax.fori_loop(0, BLOCKS, block_step, 0)
+    lax.fori_loop(0, BLOCKS, tan_step, 0)
 
     for copy in copies:
         copy.wait_send()

time: 193 us -> 193 us (level)
  no operation moved by 1% of the time
where the time goes in v9:
time: 193 us
  Pallas kernels  192 us (99%)
    pallas_call x1, Pallas kernels, per_device(): pl.pallas_call(kernel, out_shape=(pltpu.VMEM((TOK, HEADS * HD), jnp.bfloa...  191 us

profile of v9, /device:TPU:1, one launch (start us, length us, event | category | flops | bytes accessed | tf_op | source)
XLA Modules:
  0.0 192.9 jit_solution(15894629607134337366)
XLA Ops:
  0.6 190.9 %attend.1 = (bf16[128,4096]{1,0:T(8,128)(2,1)S(1)}, bf16[128,4096]{1,0:T(8,128)(2,1)S(1)}) custom-call(s32[4,16]{1,0:T(4,128)} %bitcast.1, bf16[128,4096]{1,0:T(8,128)(2,1)} %query.1, bf16[128,4096]{1,0:T(8,128)(2,1)} %keys.1, bf16[128,4096]{1,0:T(8,128)(2,1)} %values.1, bf16[128,4096]{1,0:T(8,128)(2,1)} %query_tan.1, bf16[128,4096]{1,0:T(8,128)(2,1)} %keys_tan.1, ...), custom_call_target="tpu_custom_call" | custom-call | flops 7000000000 | bytes 20971520 | tf_op jit(solution)/shard_map/attend/pallas_call | solution.py:279
  191.6 1.3 hand_on.1
